TPU v7x, 512 devices: a whole 4x4x16 slice. The times are simulated.
512 devices in a mesh: group: 16 (over y, x), dev: 32 (over z, core).
Axes of the slice: x: 4, y: 4, z: 16, core: 2. Of those that a mesh axis runs over, the one named last changes fastest.
Arguments:
- cam_jac: float32 [18, 2162688], P(None, ('group', 'dev')), may hold values from -1 to 1
- point_jac: float32 [6, 2162688], P(None, ('group', 'dev')), may hold values from -3 to 3
- residuals: float32 [2, 2162688], P(None, ('group', 'dev')), may hold values from -15 to 15
- obs_camera: int32 [2162688], P(('group', 'dev')), may hold values from 0 to 127
- obs_point: int32 [2162688], P(('group', 'dev')), may hold values from 0 to 1023
- obs_count: int32 [512, 33], P(('group', 'dev')), may hold values from 42 to 128, as said below
- cam_damp: float32 [9, 65536], P(None, ('group', 'dev')), may hold values from 0.3 to 3
- pt_damp: float32 [3, 524288], P(None, ('group', 'dev')), may hold values from 0.3 to 3
- partner_mask: int32 [32], P('dev'), may hold values from 1 to 15
Outputs:
- update: float32 [9, 65536], P(None, ('group', 'dev'))
- remainder: float32 [9, 65536], P(None, ('group', 'dev'))
Inputs may be any that keep to these rules, and one draw needn't show every extreme that they name: `obs_count`: slots at or beyond a count are padding. Every device's row holds one count equal to 128. For each index d within a partition, partitions g and g XOR partner_mask[d] are matched.
All inputs are finite; a program needn't handle non-finite values.
Results may differ from a plain program's by a relative error of at most 0.0085.
Values sent between devices are 32-bit elements; how exact they have to be, the bound alone decides.
No kernel may reach another device: no remote copies, remote signals or barrier semaphores. Data moves between devices by JAX's collectives and lax.ppermute only.
A program may use at most 64 MiB of HBM per device.

v0:
```python
import jax
import jax.numpy as jnp
from jax import lax
from jax.sharding import PartitionSpec as P

ITERS = 2


def partner_2(block, axis, distance):
    count = lax.axis_size(axis)
    route = []
    for low in range(count):
        high = low | 1 << distance
        if high != low and high < count:
            route += [(low, high), (high, low)]
    return lax.ppermute(block, axis, route)


def seg_rows(entries, indices, item_count):
    return jax.vmap(lambda single: jax.ops.segment_sum(single, indices, num_segments=item_count))(
        entries
    )


def cam_apply(cam_rows, cam_values):
    first_row = jnp.sum(cam_rows[0:9] * cam_values, axis=0)
    second_row = jnp.sum(cam_rows[9:18] * cam_values, axis=0)
    return jnp.stack([first_row, second_row])


def cam_spread(cam_rows, slot_values):
    return cam_rows[0:9] * slot_values[0:1] + cam_rows[9:18] * slot_values[1:2]


def point_apply(point_rows, point_values):
    first_row = jnp.sum(point_rows[0:3] * point_values, axis=0)
    second_row = jnp.sum(point_rows[3:6] * point_values, axis=0)
    return jnp.stack([first_row, second_row])


def point_spread(point_rows, slot_values):
    return point_rows[0:3] * slot_values[0:1] + point_rows[3:6] * slot_values[1:2]


def point_blocks(point_rows, point_ids, damping):
    item_count = damping.shape[1]
    summands = []
    for first_axis, second_axis in ((0, 0), (0, 1), (0, 2), (1, 1), (1, 2), (2, 2)):
        summands.append(
            point_rows[first_axis] * point_rows[second_axis]
            + point_rows[3 + first_axis] * point_rows[3 + second_axis]
        )
    blocks = seg_rows(jnp.stack(summands), point_ids, item_count)
    nothing = jnp.zeros_like(damping[0])
    return blocks + jnp.stack([damping[0], nothing, nothing, damping[1], nothing, damping[2]])


def solve_three(blocks, source):
    cofactor_xx = blocks[3] * blocks[5] - blocks[4] * blocks[4]
    cofactor_xy = blocks[2] * blocks[4] - blocks[1] * blocks[5]
    cofactor_xz = blocks[1] * blocks[4] - blocks[2] * blocks[3]
    cofactor_yy = blocks[0] * blocks[5] - blocks[2] * blocks[2]
    cofactor_yz = blocks[1] * blocks[2] - blocks[0] * blocks[4]
    cofactor_zz = blocks[0] * blocks[3] - blocks[1] * blocks[1]
    determinant = blocks[0] * cofactor_xx + blocks[1] * cofactor_xy + blocks[2] * cofactor_xz
    first_out = cofactor_xx * source[0] + cofactor_xy * source[1] + cofactor_xz * source[2]
    second_out = cofactor_xy * source[0] + cofactor_yy * source[1] + cofactor_yz * source[2]
    third_out = cofactor_xz * source[0] + cofactor_yz * source[1] + cofactor_zz * source[2]
    return jnp.stack([first_out, second_out, third_out]) / determinant


def across(values, partner, swapper, bit_count):
    for bit_index in range(bit_count):
        moved = swapper(values, bit_index)
        chosen = jnp.bitwise_and(jnp.right_shift(partner, bit_index), 1) == 1
        values = jnp.where(chosen, moved, values)
    return values


def on_device(
    cam_jac, point_jac, residuals, obs_camera, obs_point, obs_count, cam_damp, pt_damp, partner_mask
):
    members = lax.axis_size("dev")
    bit_count = lax.axis_size("group").bit_length() - 1
    block_count = members + 1
    slot_total = cam_jac.shape[1]
    slot_size = slot_total // block_count
    inner_total = members * slot_size
    cam_count = cam_damp.shape[1]
    point_count = pt_damp.shape[1]
    partner = partner_mask[0]
    live = (
        (jnp.arange(slot_size, dtype=jnp.int32)[None, :] < obs_count[0][:, None])
        .reshape(-1)
        .astype(jnp.float32)
    )
    cam_rows = cam_jac * live
    point_rows = point_jac * live
    blocks = point_blocks(point_rows, obs_point, pt_damp)

    def point_side(moved):
        pulled = solve_three(
            blocks, seg_rows(point_spread(point_rows, moved), obs_point, point_count)
        )
        return moved - point_apply(point_rows, pulled[:, obs_point])

    reduced = point_side(residuals)
    payload = jnp.concatenate([cam_rows, reduced, obs_camera.astype(jnp.float32)[None, :]], 0)
    arrived_inner = lax.all_to_all(
        payload[:, :inner_total], "dev", split_axis=1, concat_axis=1, tiled=True
    )
    arrived_outer = across(
        payload[:, inner_total:],
        partner,
        lambda values, bit_index: partner_2(values, "group", bit_index),
        bit_count,
    )
    arrived = jnp.concatenate([arrived_inner, arrived_outer], 1)
    owned_rows = arrived[0:18]
    owned_ids = arrived[20].astype(jnp.int32)
    gradient = -seg_rows(cam_spread(owned_rows, arrived[18:20]), owned_ids, cam_count)
    diagonal = cam_damp + seg_rows(
        owned_rows[0:9] ** 2 + owned_rows[9:18] ** 2, owned_ids, cam_count
    )

    def schur(direction):
        moved = cam_apply(owned_rows, direction[:, owned_ids])
        sent_inner = lax.all_to_all(
            moved[:, :inner_total], "dev", split_axis=1, concat_axis=1, tiled=True
        )
        sent_outer = across(
            moved[:, inner_total:],
            partner,
            lambda values, bit_index: partner_2(values, "group", bit_index),
            bit_count,
        )
        kept = point_side(jnp.concatenate([sent_inner, sent_outer], 1))
        back_inner = lax.all_to_all(
            kept[:, :inner_total], "dev", split_axis=1, concat_axis=1, tiled=True
        )
        back_outer = across(
            kept[:, inner_total:],
            partner,
            lambda values, bit_index: partner_2(values, "group", bit_index),
            bit_count,
        )
        returned = jnp.concatenate([back_inner, back_outer], 1)
        return cam_damp * direction + seg_rows(
            cam_spread(owned_rows, returned), owned_ids, cam_count
        )

    precond = 1.0 / diagonal
    update = jnp.zeros_like(gradient)
    remainder = gradient
    scaled = precond * remainder
    direction = scaled
    norm_now = lax.psum(jnp.sum(remainder * scaled), ("group", "dev"))
    for step_index in range(ITERS):
        image = schur(direction)
        curvature = lax.psum(jnp.sum(direction * image), ("group", "dev"))
        step_size = norm_now / curvature
        update = update + step_size * direction
        remainder = remainder - step_size * image
        if step_index + 1 < ITERS:
            scaled = precond * remainder
            norm_next = lax.psum(jnp.sum(remainder * scaled), ("group", "dev"))
            direction = scaled + norm_next / norm_now * direction
            norm_now = norm_next
    return (update, remainder)


def solution(mesh):
    return jax.shard_map(
        on_device,
        mesh=mesh,
        in_specs=(
            P(None, ("group", "dev")),
            P(None, ("group", "dev")),
            P(None, ("group", "dev")),
            P(("group", "dev")),
            P(("group", "dev")),
            P(("group", "dev"), None),
            P(None, ("group", "dev")),
            P(None, ("group", "dev")),
            P("dev"),
        ),
        out_specs=(P(None, ("group", "dev")), P(None, ("group", "dev"))),
        check_vma=False,
    )
```

profile of v0, /device:TPU:1, one launch (start us, length us, event | category | flops | bytes accessed | tf_op | source)
XLA Modules:
  0.0 864.4 jit_solution(16352821904402981239)
XLA Ops:
  31.1 25.9 %scatter_fusion = f32[6,1024]{0,1:T(8,128)S(1)} fusion(f32[6,1024]{0,1:T(8,128)S(1)} %copy.265, s32[4224]{0:T(1024)S(1)} %copy-done.11, f32[4224,6]{1,0:T(8,128)} %copy.266), kind=kCustom, calls=%fused_computation.5 | custom fusion | flops 25344 | bytes 321024 | tf_op jit(solution)/shard_map/vmap()/scatter-add | solution.py:20
  64.6 28.7 %scatter_custom_fusion.1 = f32[3,1024]{0,1:T(8,128)S(1)} fusion(s32[4224]{0:T(1024)S(1)} %copy-done.11, f32[6,4224]{0,1:T(8,128)S(1)} %broadcast_multiply_fusion, f32[4224]{0:T(1024)S(1)} %get-tuple-element.37, f32[4224]{0:T(1024)S(1)} %get-tuple-element.36, f32[]{:T(128)} %constant.12.clone.1), kind=kCustom, calls=%fused_computation.45 | custom fusion | flops 50688 | bytes 4378628 | tf_op jit(solution)/shard_map/vmap()/scatter-add | solution.py:20
  98.9 8.7 %gather_fusion = f32[4224,3]{1,0:T(8,128)} fusion(f32[3,1024]{0,1:T(8,128)S(1)} %copy.276, s32[5120]{0:T(1024)S(1)} %pad_clamp_fusion.1), kind=kCustom, calls=%fused_computation | custom fusion | bytes 118272 | tf_op jit(solution)/shard_map/gather | solution.py:105
  112.4 16.7 %all-to-all-start = ((f32[21,32,128]{2,0,1:T(8,128)}), f32[21,32,128]{2,0,1:T(8,128)S(1)}, u32[]{:S(2)}, u32[]{:S(2)}) async-start(f32[21,32,128]{2,0,1:T(8,128)} %copy.277), calls=%async_computation | async-start | bytes 786432 | tf_op jit(solution)/shard_map/all_to_all | solution.py:109
  161.9 26.1 %scatter_custom_fusion.3 = f32[9,128]{0,1:T(8,128)S(1)} fusion(f32[9,128]{0,1:T(8,128)S(1)} %copy.314, s32[4224]{0:T(1024)S(1)} %reduce.2, f32[9,4224]{0,1:T(8,128)} %copy.304, f32[9,4224]{0,1:T(8,128)} %copy.303), kind=kCustom, calls=%fused_computation.37 | custom fusion | flops 152064 | bytes 308736 | tf_op jit(solution)/shard_map/vmap()/scatter-add | solution.py:20
  188.0 28.5 %scatter_custom_fusion.2 = f32[9,128]{0,1:T(8,128)S(1)} fusion(s32[4224]{0:T(1024)S(1)} %reduce.2, f32[9,4224]{0,1:T(8,128)} %copy.304, f32[9,4224]{0,1:T(8,128)} %copy.303, f32[4224]{0:T(1024)S(1)} %get-tuple-element.25, f32[4224]{0:T(1024)S(1)} %get-tuple-element.24, f32[]{:T(128)} %constant.12.clone.1), kind=kCustom, calls=%fused_computation.39 | custom fusion | flops 152064 | bytes 349700 | tf_op jit(solution)/shard_map/vmap()/scatter-add | solution.py:20
  216.6 8.7 %gather_fusion.1 = f32[4224,9]{1,0:T(8,128)} fusion(f32[9,128]{0,1:T(8,128)S(1)} %get-tuple-element.47, s32[5120]{0:T(1024)S(1)} %pad_clamp_fusion), kind=kCustom, calls=%fused_computation.1 | custom fusion | bytes 321024 | tf_op jit(solution)/shard_map/gather | solution.py:127
  249.4 13.3 %all-to-all-start.1 = ((f32[2,32,128]{2,0,1:T(2,128)}), f32[2,32,128]{2,0,1:T(2,128)S(1)}, u32[]{:S(2)}, u32[]{:S(2)}) async-start(f32[2,32,128]{2,0,1:T(2,128)} %fusion.73), calls=%async_computation.1 | async-start | bytes 65536 | tf_op jit(solution)/shard_map/all_to_all | solution.py:128
  262.7 12.1 %all-to-all-done.1 = f32[2,32,128]{2,0,1:T(2,128)S(1)} async-done(((f32[2,32,128]{2,0,1:T(2,128)}), f32[2,32,128]{2,0,1:T(2,128)S(1)}, u32[]{:S(2)}, u32[]{:S(2)}) %all-to-all-start.1) | async-done | bytes 32800 | tf_op jit(solution)/shard_map/all_to_all | solution.py:128
  275.4 28.8 %scatter_custom_fusion.4 = f32[3,1024]{0,1:T(8,128)S(1)} fusion(s32[4224]{0:T(1024)} %param.13, f32[6,4224]{0,1:T(8,128)S(1)} %broadcast_multiply_fusion, f32[4224]{0:T(1024)S(1)} %get-tuple-element.35, f32[4224]{0:T(1024)S(1)} %get-tuple-element.34, f32[]{:T(128)} %constant.12.clone.1), kind=kCustom, calls=%fused_computation.31 | custom fusion | flops 50688 | bytes 4379136 | tf_op jit(solution)/shard_map/vmap()/scatter-add | solution.py:20
  309.8 9.5 %gather_fusion.2 = f32[4224,3]{1,0:T(8,128)} fusion(f32[3,1024]{0,1:T(8,128)S(1)} %copy.286, s32[5120]{0:T(1024)} %copy-done.4), kind=kCustom, calls=%fused_computation.2 | custom fusion | bytes 118272 | tf_op jit(solution)/shard_map/gather | solution.py:105
  348.3 12.3 %all-to-all-done.2 = f32[2,32,128]{2,0,1:T(2,128)S(1)} async-done(((f32[2,32,128]{2,0,1:T(2,128)}), f32[2,32,128]{2,0,1:T(2,128)S(1)}, u32[]{:S(2)}, u32[]{:S(2)}) %all-to-all-start.2) | async-done | bytes 32800 | tf_op jit(solution)/shard_map/all_to_all | solution.py:138
  360.7 29.0 %scatter_custom_fusion.5 = f32[9,128]{0,1:T(8,128)S(1)} fusion(f32[9,128]{0,1:T(8,128)S(1)} %get-tuple-element.46, s32[4224]{0:T(1024)} %copy-done.17, f32[9,4224]{0,1:T(8,128)} %copy.304, f32[9,4224]{0,1:T(8,128)} %copy.303, f32[4224]{0:T(1024)S(1)} %get-tuple-element.33, f32[4224]{0:T(1024)S(1)} %get-tuple-element.32), kind=kCustom, calls=%fused_computation.25 | custom fusion | flops 152064 | bytes 4370944 | tf_op jit(solution)/shard_map/vmap()/scatter-add | solution.py:20
  390.3 101.9 %all-reduce = (f32[]{:T(128)}, f32[]{:T(128)}) all-reduce(f32[]{:T(128)} %get-tuple-element.27, f32[]{:T(128)} %get-tuple-element.26), channel_id=1, replica_groups=mesh['group'=16,'dev'=32] {'group','dev'}, use_global_device_ids=true, to_apply=%region_7.8 | all-reduce | flops 2 | bytes 16 | tf_op jit(solution)/shard_map/psum | solution.py:157
  494.1 99.5 %psum.30 = f32[]{:T(128)} all-reduce(f32[]{:T(128)} %get-tuple-element.42), channel_id=1, replica_groups=mesh['group'=16,'dev'=32] {'group','dev'}, use_global_device_ids=true, to_apply=%region_17.18 | all-reduce | flops 1 | bytes 8 | tf_op jit(solution)/shard_map/psum | solution.py:166
  595.0 8.7 %gather_fusion.3 = f32[4224,9]{1,0:T(8,128)} fusion(f32[9,128]{0,1:T(8,128)S(1)} %get-tuple-element.41, s32[5120]{0:T(1024)S(1)} %copy-done.9), kind=kCustom, calls=%fused_computation.3 | custom fusion | bytes 321024 | tf_op jit(solution)/shard_map/gather | solution.py:127
  626.2 10.0 %all-to-all-start.3 = ((f32[2,32,128]{2,0,1:T(2,128)}), f32[2,32,128]{2,0,1:T(2,128)S(1)}, u32[]{:S(2)}, u32[]{:S(2)}) async-start(f32[2,32,128]{2,0,1:T(2,128)} %fusion.71), calls=%async_computation.3 | async-start | bytes 65536 | tf_op jit(solution)/shard_map/all_to_all | solution.py:128
  636.2 12.1 %all-to-all-done.3 = f32[2,32,128]{2,0,1:T(2,128)S(1)} async-done(((f32[2,32,128]{2,0,1:T(2,128)}), f32[2,32,128]{2,0,1:T(2,128)S(1)}, u32[]{:S(2)}, u32[]{:S(2)}) %all-to-all-start.3) | async-done | bytes 32800 | tf_op jit(solution)/shard_map/all_to_all | solution.py:128
  648.4 29.0 %scatter_custom_fusion.6 = f32[3,1024]{0,1:T(8,128)S(1)} fusion(s32[4224]{0:T(1024)} %param.13, f32[6,4224]{0,1:T(8,128)S(1)} %broadcast_multiply_fusion, f32[4224]{0:T(1024)S(1)} %get-tuple-element.31, f32[4224]{0:T(1024)S(1)} %get-tuple-element.30, f32[]{:T(128)} %constant.12.clone.1), kind=kCustom, calls=%fused_computation.19 | custom fusion | flops 50688 | bytes 4379136 | tf_op jit(solution)/shard_map/vmap()/scatter-add | solution.py:20
  681.7 8.7 %gather_fusion.4 = f32[4224,3]{1,0:T(8,128)} fusion(f32[3,1024]{0,1:T(8,128)S(1)} %copy.291, s32[5120]{0:T(1024)S(1)} %copy-done.5), kind=kCustom, calls=%fused_computation.4 | custom fusion | bytes 118272 | tf_op jit(solution)/shard_map/gather | solution.py:105
  712.5 8.3 all-to-all-start.4
  720.9 12.3 %all-to-all-done.4 = f32[2,32,128]{2,0,1:T(2,128)S(1)} async-done(((f32[2,32,128]{2,0,1:T(2,128)}), f32[2,32,128]{2,0,1:T(2,128)S(1)}, u32[]{:S(2)}, u32[]{:S(2)}) %all-to-all-start.4) | async-done | bytes 32800 | tf_op jit(solution)/shard_map/all_to_all | solution.py:138
  733.2 28.6 %scatter_custom_fusion.7 = f32[9,128]{0,1:T(8,128)S(1)} fusion(f32[9,128]{0,1:T(8,128)S(1)} %get-tuple-element.40, s32[4224]{0:T(1024)} %copy-done.17, f32[9,4224]{0,1:T(8,128)} %copy.304, f32[9,4224]{0,1:T(8,128)} %copy.303, f32[4224]{0:T(1024)S(1)} %get-tuple-element.29, f32[4224]{0:T(1024)S(1)} %get-tuple-element.28), kind=kCustom, calls=%fused_computation.13 | custom fusion | flops 152064 | bytes 4370944 | tf_op jit(solution)/shard_map/vmap()/scatter-add | solution.py:20
  762.5 99.0 %psum.31 = f32[]{:T(128)} all-reduce(f32[]{:T(128)} %multiply_reduce_fusion), channel_id=1, replica_groups=mesh['group'=16,'dev'=32] {'group','dev'}, use_global_device_ids=true, to_apply=%region_25.26 | all-reduce | flops 1 | bytes 8 | tf_op jit(solution)/shard_map/psum | solution.py:160
  (216 shorter events, 191.4 us)
Async XLA Ops:
  112.4 44.7 %all-to-all-start = ((f32[21,32,128]{2,0,1:T(8,128)}), f32[21,32,128]{2,0,1:T(8,128)S(1)}, u32[]{:S(2)}, u32[]{:S(2)}) async-start(f32[21,32,128]{2,0,1:T(8,128)} %copy.277), calls=%async_computation | async-start | bytes 786432 | tf_op jit(solution)/shard_map/all_to_all | solution.py:109
  129.1 4.4 collective-permute-start
  133.6 6.2 collective-permute-start.1
  139.8 4.7 collective-permute-start.2
  144.5 5.9 collective-permute-start.3
  229.5 4.3 collective-permute-start.4
  233.8 5.8 collective-permute-start.5
  239.6 4.3 collective-permute-start.6
  243.9 18.8 %collective-permute-start.7 = (f32[2,128]{1,0:T(2,128)S(1)}, f32[2,128]{1,0:T(2,128)S(1)}, u32[]{:S(2)}, u32[]{:S(2)}) collective-permute-start(f32[2,128]{1,0:T(2,128)S(1)} %broadcast_select_fusion.15), channel_id=1, source_target_pairs={{0,256},{256,0},{32,288},{288,32},{64,320},{320,64},{96,352},{352,... | collective-permute-start | bytes 3080 | tf_op jit(solution)/shard_map/ppermute | solution.py:16
  249.4 25.4 %all-to-all-start.1 = ((f32[2,32,128]{2,0,1:T(2,128)}), f32[2,32,128]{2,0,1:T(2,128)S(1)}, u32[]{:S(2)}, u32[]{:S(2)}) async-start(f32[2,32,128]{2,0,1:T(2,128)} %fusion.73), calls=%async_computation.1 | async-start | bytes 65536 | tf_op jit(solution)/shard_map/all_to_all | solution.py:128
  322.8 4.3 collective-permute-start.8
  327.1 5.8 collective-permute-start.9
  332.9 4.3 collective-permute-start.10
  337.2 11.1 %collective-permute-start.11 = (f32[2,128]{1,0:T(2,128)S(1)}, f32[2,128]{1,0:T(2,128)S(1)}, u32[]{:S(2)}, u32[]{:S(2)}) collective-permute-start(f32[2,128]{1,0:T(2,128)S(1)} %broadcast_select_fusion.14), channel_id=1, source_target_pairs={{0,256},{256,0},{32,288},{288,32},{64,320},{320,64},{96,352},{352,... | collective-permute-start | bytes 3080 | tf_op jit(solution)/shard_map/ppermute | solution.py:16
  340.3 20.3 %all-to-all-start.2 = ((f32[2,32,128]{2,0,1:T(2,128)}), f32[2,32,128]{2,0,1:T(2,128)S(1)}, u32[]{:S(2)}, u32[]{:S(2)}) async-start(f32[2,32,128]{2,0,1:T(2,128)} %slice_bitcast_fusion.1), calls=%async_computation.2 | async-start | bytes 65536 | tf_op jit(solution)/shard_map/all_to_all | solution.py:138
  607.9 4.3 collective-permute-start.12
  612.2 5.8 collective-permute-start.13
  618.1 4.3 collective-permute-start.14
  622.4 13.8 %collective-permute-start.15 = (f32[2,128]{1,0:T(2,128)S(1)}, f32[2,128]{1,0:T(2,128)S(1)}, u32[]{:S(2)}, u32[]{:S(2)}) collective-permute-start(f32[2,128]{1,0:T(2,128)S(1)} %broadcast_select_fusion.13), channel_id=1, source_target_pairs={{0,256},{256,0},{32,288},{288,32},{64,320},{320,64},{96,352},{352,... | collective-permute-start | bytes 3080 | tf_op jit(solution)/shard_map/ppermute | solution.py:16
  626.2 22.1 %all-to-all-start.3 = ((f32[2,32,128]{2,0,1:T(2,128)}), f32[2,32,128]{2,0,1:T(2,128)S(1)}, u32[]{:S(2)}, u32[]{:S(2)}) async-start(f32[2,32,128]{2,0,1:T(2,128)} %fusion.71), calls=%async_computation.3 | async-start | bytes 65536 | tf_op jit(solution)/shard_map/all_to_all | solution.py:128
  693.9 4.3 collective-permute-start.16
  698.2 5.8 collective-permute-start.17
  708.4 12.5 %collective-permute-start.19 = (f32[2,128]{1,0:T(2,128)S(1)}, f32[2,128]{1,0:T(2,128)S(1)}, u32[]{:S(2)}, u32[]{:S(2)}) collective-permute-start(f32[2,128]{1,0:T(2,128)S(1)} %broadcast_select_fusion.12), channel_id=1, source_target_pairs={{0,256},{256,0},{32,288},{288,32},{64,320},{320,64},{96,352},{352,... | collective-permute-start | bytes 3080 | tf_op jit(solution)/shard_map/ppermute | solution.py:16
  712.5 20.6 %all-to-all-start.4 = ((f32[2,32,128]{2,0,1:T(2,128)}), f32[2,32,128]{2,0,1:T(2,128)S(1)}, u32[]{:S(2)}, u32[]{:S(2)}) async-start(f32[2,32,128]{2,0,1:T(2,128)} %slice_bitcast_fusion), calls=%async_computation.4 | async-start | bytes 65536 | tf_op jit(solution)/shard_map/all_to_all | solution.py:138
  (23 other events, 675.3 us)
where the time goes:
time: 873 us; the launch traced here: 864 us
  blocking collectives  300 us (34%)
  other arithmetic  254 us (29%)
  starting transfers between devices  122 us (14%)
  local copies, waits for them, and re-layouts  99.9 us (11%)
  waiting for transfers between devices  81.4 us (9%)
    scatter-add x8, other arithmetic, seg_rows(): jax.ops.segment_sum(single, indices, num_segments=item_count)  225 us
    psum x1, blocking collectives, on_device(): norm_now = lax.psum(jnp.sum(remainder * scaled), ('group', 'dev'))  102 us
    psum x1, blocking collectives, on_device(): norm_next = lax.psum(jnp.sum(remainder * scaled), ('group', 'dev'))  99.5 us
    psum x1, blocking collectives, on_device(): curvature = lax.psum(jnp.sum(direction * image), ('group', 'dev'))  99 us
    ppermute x20, starting transfers between devices, partner_2(): return lax.ppermute(block, axis, route)  66 us
    gather x3, local copies, waits for them, and re-layouts, point_side(): return moved - point_apply(point_rows, pulled[:, obs_point])  26.9 us
    ppermute x20, waiting for transfers between devices, partner_2(): return lax.ppermute(block, axis, route)  26.1 us
    all_to_all x2, waiting for transfers between devices, schur(): lax.all_to_all(kept[:, :inner_total], 'dev', split_axis=1, concat_axis=1,...  24.5 us
  transfers between devices with their start and end apart: 25, of which 21 were waited for; matrix products, arithmetic and copies ran while one was open for 0% of the time, Pallas kernels for 0%

commit v1 on v0

--- a/solution.py
+++ b/solution.py
@@ -4,6 +4,13 @@
 from jax.sharding import PartitionSpec as P
 
 ITERS = 2
+
+
+def step_on_the_rows(arr):
+    b_next = lax.axis_size("dev")
+    after = lax.all_to_all(jnp.stack(jnp.split(arr, b_next, axis=1)), "dev", 0, 0)
+    now = jnp.concatenate(after, axis=1)
+    return now
 
 
 def partner_2(block, axis, distance):
@@ -135,9 +142,7 @@
             bit_count,
         )
         kept = point_side(jnp.concatenate([sent_inner, sent_outer], 1))
-        back_inner = lax.all_to_all(
-            kept[:, :inner_total], "dev", split_axis=1, concat_axis=1, tiled=True
-        )
+        back_inner = step_on_the_rows(kept[:, :inner_total])
         back_outer = across(
             kept[:, inner_total:],
             partner,

time: 873 us -> 905 us (1.037)
  local copies, waits for them, and re-layouts: 99.9 us -> 135 us
    unnamed x69 -> x131, local copies, waits for them, and re-layouts: 22.7 us -> 58.2 us
  transfers between devices with their start and end apart: 25 -> 25, of which waited for: 21 -> 21; matrix products, arithmetic and copies ran while one was open for 0% -> 1% of each run, Pallas kernels for 0% -> 0%
where the time goes in v1:
time: 905 us; the launch traced here: 896 us
  blocking collectives  300 us (33%)
  other arithmetic  254 us (28%)
  local copies, waits for them, and re-layouts  135 us (15%)
  starting transfers between devices  122 us (13%)
  waiting for transfers between devices  78 us (9%)
    scatter-add x8, other arithmetic, seg_rows(): jax.ops.segment_sum(single, indices, num_segments=item_count)  225 us
    psum x1, blocking collectives, on_device(): norm_now = lax.psum(jnp.sum(remainder * scaled), ('group', 'dev'))  102 us
    psum x1, blocking collectives, on_device(): norm_next = lax.psum(jnp.sum(remainder * scaled), ('group', 'dev'))  99.5 us
    psum x1, blocking collectives, on_device(): curvature = lax.psum(jnp.sum(direction * image), ('group', 'dev'))  99 us
    ppermute x20, starting transfers between devices, partner_2(): return lax.ppermute(block, axis, route)  65.9 us
    unnamed x131, local copies, waits for them, and re-layouts  58.2 us
    gather x3, local copies, waits for them, and re-layouts, point_side(): return moved - point_apply(point_rows, pulled[:, obs_point])  26.9 us
    all_to_all x2, waiting for transfers between devices, step_on_the_rows(): lax.all_to_all(jnp.stack(jnp.split(arr, b_next, axis=1)), 'dev', 0, 0)  24.5 us
  transfers between devices with their start and end apart: 25, of which 21 were waited for; matrix products, arithmetic and copies ran while one was open for 1% of the time, Pallas kernels for 0%

profile of v1, /device:TPU:1, one launch (start us, length us, event | category | flops | bytes accessed | tf_op | source)
XLA Modules:
  0.0 896.4 jit_solution(6077536501126430697)
XLA Ops:
  31.1 25.9 %scatter_fusion = f32[6,1024]{0,1:T(8,128)S(1)} fusion(f32[6,1024]{0,1:T(8,128)S(1)} %copy.265, s32[4224]{0:T(1024)S(1)} %copy-done.11, f32[4224,6]{1,0:T(8,128)} %copy.266), kind=kCustom, calls=%fused_computation.5 | custom fusion | flops 25344 | bytes 321024 | tf_op jit(solution)/shard_map/vmap()/scatter-add | solution.py:27
  64.6 28.7 %scatter_custom_fusion.1 = f32[3,1024]{0,1:T(8,128)S(1)} fusion(s32[4224]{0:T(1024)S(1)} %copy-done.11, f32[6,4224]{0,1:T(8,128)S(1)} %broadcast_multiply_fusion, f32[4224]{0:T(1024)S(1)} %get-tuple-element.37, f32[4224]{0:T(1024)S(1)} %get-tuple-element.36, f32[]{:T(128)} %constant.12.clone.1), kind=kCustom, calls=%fused_computation.45 | custom fusion | flops 50688 | bytes 4378628 | tf_op jit(solution)/shard_map/vmap()/scatter-add | solution.py:27
  98.9 8.7 gather_fusion
  112.4 16.7 %all-to-all-start = ((f32[21,32,128]{2,0,1:T(8,128)}), f32[21,32,128]{2,0,1:T(8,128)S(1)}, u32[]{:S(2)}, u32[]{:S(2)}) async-start(f32[21,32,128]{2,0,1:T(8,128)} %copy.277), calls=%async_computation | async-start | bytes 786432 | tf_op jit(solution)/shard_map/all_to_all | solution.py:116
  161.9 26.1 %scatter_custom_fusion.3 = f32[9,128]{0,1:T(8,128)S(1)} fusion(f32[9,128]{0,1:T(8,128)S(1)} %copy.314, s32[4224]{0:T(1024)S(1)} %reduce.2, f32[9,4224]{0,1:T(8,128)} %copy.304, f32[9,4224]{0,1:T(8,128)} %copy.303), kind=kCustom, calls=%fused_computation.37 | custom fusion | flops 152064 | bytes 308736 | tf_op jit(solution)/shard_map/vmap()/scatter-add | solution.py:27
  188.0 28.5 %scatter_custom_fusion.2 = f32[9,128]{0,1:T(8,128)S(1)} fusion(s32[4224]{0:T(1024)S(1)} %reduce.2, f32[9,4224]{0,1:T(8,128)} %copy.304, f32[9,4224]{0,1:T(8,128)} %copy.303, f32[4224]{0:T(1024)S(1)} %get-tuple-element.25, f32[4224]{0:T(1024)S(1)} %get-tuple-element.24, f32[]{:T(128)} %constant.12.clone.1), kind=kCustom, calls=%fused_computation.39 | custom fusion | flops 152064 | bytes 349700 | tf_op jit(solution)/shard_map/vmap()/scatter-add | solution.py:27
  216.6 8.7 gather_fusion.1
  249.4 13.3 %all-to-all-start.1 = ((f32[2,32,128]{2,0,1:T(2,128)}), f32[2,32,128]{2,0,1:T(2,128)S(1)}, u32[]{:S(2)}, u32[]{:S(2)}) async-start(f32[2,32,128]{2,0,1:T(2,128)} %fusion.73), calls=%async_computation.1 | async-start | bytes 65536 | tf_op jit(solution)/shard_map/all_to_all | solution.py:135
  262.7 12.1 %all-to-all-done.1 = f32[2,32,128]{2,0,1:T(2,128)S(1)} async-done(((f32[2,32,128]{2,0,1:T(2,128)}), f32[2,32,128]{2,0,1:T(2,128)S(1)}, u32[]{:S(2)}, u32[]{:S(2)}) %all-to-all-start.1) | async-done | bytes 32800 | tf_op jit(solution)/shard_map/all_to_all | solution.py:135
  275.4 28.8 %scatter_custom_fusion.4 = f32[3,1024]{0,1:T(8,128)S(1)} fusion(s32[4224]{0:T(1024)} %param.13, f32[6,4224]{0,1:T(8,128)S(1)} %broadcast_multiply_fusion, f32[4224]{0:T(1024)S(1)} %get-tuple-element.35, f32[4224]{0:T(1024)S(1)} %get-tuple-element.34, f32[]{:T(128)} %constant.12.clone.1), kind=kCustom, calls=%fused_computation.31 | custom fusion | flops 50688 | bytes 4379136 | tf_op jit(solution)/shard_map/vmap()/scatter-add | solution.py:27
  309.8 9.5 %gather_fusion.2 = f32[4224,3]{1,0:T(8,128)} fusion(f32[3,1024]{0,1:T(8,128)S(1)} %copy.286, s32[5120]{0:T(1024)} %copy-done.4), kind=kCustom, calls=%fused_computation.2 | custom fusion | bytes 118272 | tf_op jit(solution)/shard_map/gather | solution.py:112
  364.3 12.3 %all-to-all-done.2 = f32[32,2,128]{2,1,0:T(2,128)S(1)} async-done(((f32[32,2,128]{2,1,0:T(2,128)}), f32[32,2,128]{2,1,0:T(2,128)S(1)}, u32[]{:S(2)}, u32[]{:S(2)}) %all-to-all-start.2) | async-done | bytes 32800 | tf_op jit(solution)/shard_map/all_to_all | solution.py:11
  376.7 29.0 %scatter_custom_fusion.5 = f32[9,128]{0,1:T(8,128)S(1)} fusion(f32[9,128]{0,1:T(8,128)S(1)} %get-tuple-element.46, s32[4224]{0:T(1024)} %copy-done.17, f32[9,4224]{0,1:T(8,128)} %copy.304, f32[9,4224]{0,1:T(8,128)} %copy.303, f32[4224]{0:T(1024)S(1)} %get-tuple-element.33, f32[4224]{0:T(1024)S(1)} %get-tuple-element.32), kind=kCustom, calls=%fused_computation.25 | custom fusion | flops 152064 | bytes 4370944 | tf_op jit(solution)/shard_map/vmap()/scatter-add | solution.py:27
  406.3 101.9 %all-reduce = (f32[]{:T(128)}, f32[]{:T(128)}) all-reduce(f32[]{:T(128)} %get-tuple-element.27, f32[]{:T(128)} %get-tuple-element.26), channel_id=1, replica_groups=mesh['group'=16,'dev'=32] {'group','dev'}, use_global_device_ids=true, to_apply=%region_7.8 | all-reduce | flops 2 | bytes 16 | tf_op jit(solution)/shard_map/psum | solution.py:162
  510.1 99.5 %psum.30 = f32[]{:T(128)} all-reduce(f32[]{:T(128)} %get-tuple-element.42), channel_id=1, replica_groups=mesh['group'=16,'dev'=32] {'group','dev'}, use_global_device_ids=true, to_apply=%region_17.18 | all-reduce | flops 1 | bytes 8 | tf_op jit(solution)/shard_map/psum | solution.py:171
  611.0 8.7 gather_fusion.3
  642.2 10.0 %all-to-all-start.3 = ((f32[2,32,128]{2,0,1:T(2,128)}), f32[2,32,128]{2,0,1:T(2,128)S(1)}, u32[]{:S(2)}, u32[]{:S(2)}) async-start(f32[2,32,128]{2,0,1:T(2,128)} %fusion.71), calls=%async_computation.3 | async-start | bytes 65536 | tf_op jit(solution)/shard_map/all_to_all | solution.py:135
  652.2 12.1 %all-to-all-done.3 = f32[2,32,128]{2,0,1:T(2,128)S(1)} async-done(((f32[2,32,128]{2,0,1:T(2,128)}), f32[2,32,128]{2,0,1:T(2,128)S(1)}, u32[]{:S(2)}, u32[]{:S(2)}) %all-to-all-start.3) | async-done | bytes 32800 | tf_op jit(solution)/shard_map/all_to_all | solution.py:135
  664.4 29.0 %scatter_custom_fusion.6 = f32[3,1024]{0,1:T(8,128)S(1)} fusion(s32[4224]{0:T(1024)} %param.13, f32[6,4224]{0,1:T(8,128)S(1)} %broadcast_multiply_fusion, f32[4224]{0:T(1024)S(1)} %get-tuple-element.31, f32[4224]{0:T(1024)S(1)} %get-tuple-element.30, f32[]{:T(128)} %constant.12.clone.1), kind=kCustom, calls=%fused_computation.19 | custom fusion | flops 50688 | bytes 4379136 | tf_op jit(solution)/shard_map/vmap()/scatter-add | solution.py:27
  697.7 8.7 gather_fusion.4
  744.5 8.3 all-to-all-start.4
  752.9 12.3 %all-to-all-done.4 = f32[32,2,128]{2,1,0:T(2,128)S(1)} async-done(((f32[32,2,128]{2,1,0:T(2,128)}), f32[32,2,128]{2,1,0:T(2,128)S(1)}, u32[]{:S(2)}, u32[]{:S(2)}) %all-to-all-start.4) | async-done | bytes 32800 | tf_op jit(solution)/shard_map/all_to_all | solution.py:11
  765.2 28.6 %scatter_custom_fusion.7 = f32[9,128]{0,1:T(8,128)S(1)} fusion(f32[9,128]{0,1:T(8,128)S(1)} %get-tuple-element.40, s32[4224]{0:T(1024)} %copy-done.17, f32[9,4224]{0,1:T(8,128)} %copy.304, f32[9,4224]{0,1:T(8,128)} %copy.303, f32[4224]{0:T(1024)S(1)} %get-tuple-element.29, f32[4224]{0:T(1024)S(1)} %get-tuple-element.28), kind=kCustom, calls=%fused_computation.13 | custom fusion | flops 152064 | bytes 4370944 | tf_op jit(solution)/shard_map/vmap()/scatter-add | solution.py:27
  794.5 99.0 %psum.31 = f32[]{:T(128)} all-reduce(f32[]{:T(128)} %multiply_reduce_fusion), channel_id=1, replica_groups=mesh['group'=16,'dev'=32] {'group','dev'}, use_global_device_ids=true, to_apply=%region_25.26 | all-reduce | flops 1 | bytes 8 | tf_op jit(solution)/shard_map/psum | solution.py:165
  (278 shorter events, 223.4 us)
Async XLA Ops:
  112.4 44.7 %all-to-all-start = ((f32[21,32,128]{2,0,1:T(8,128)}), f32[21,32,128]{2,0,1:T(8,128)S(1)}, u32[]{:S(2)}, u32[]{:S(2)}) async-start(f32[21,32,128]{2,0,1:T(8,128)} %copy.277), calls=%async_computation | async-start | bytes 786432 | tf_op jit(solution)/shard_map/all_to_all | solution.py:116
  129.1 4.4 collective-permute-start
  133.6 6.2 collective-permute-start.1
  139.8 4.7 collective-permute-start.2
  144.5 5.9 collective-permute-start.3
  229.5 4.3 collective-permute-start.4
  233.8 5.8 collective-permute-start.5
  239.6 4.3 collective-permute-start.6
  243.9 18.8 %collective-permute-start.7 = (f32[2,128]{1,0:T(2,128)S(1)}, f32[2,128]{1,0:T(2,128)S(1)}, u32[]{:S(2)}, u32[]{:S(2)}) collective-permute-start(f32[2,128]{1,0:T(2,128)S(1)} %broadcast_select_fusion.15), channel_id=1, source_target_pairs={{0,256},{256,0},{32,288},{288,32},{64,320},{320,64},{96,352},{352,... | collective-permute-start | bytes 3080 | tf_op jit(solution)/shard_map/ppermute | solution.py:23
  249.4 25.4 %all-to-all-start.1 = ((f32[2,32,128]{2,0,1:T(2,128)}), f32[2,32,128]{2,0,1:T(2,128)S(1)}, u32[]{:S(2)}, u32[]{:S(2)}) async-start(f32[2,32,128]{2,0,1:T(2,128)} %fusion.73), calls=%async_computation.1 | async-start | bytes 65536 | tf_op jit(solution)/shard_map/all_to_all | solution.py:135
  338.8 4.3 collective-permute-start.8
  343.1 5.8 collective-permute-start.9
  349.0 4.3 collective-permute-start.10
  353.3 11.0 %collective-permute-start.11 = (f32[2,128]{1,0:T(2,128)S(1)}, f32[2,128]{1,0:T(2,128)S(1)}, u32[]{:S(2)}, u32[]{:S(2)}) collective-permute-start(f32[2,128]{1,0:T(2,128)S(1)} %broadcast_select_fusion.14), channel_id=1, source_target_pairs={{0,256},{256,0},{32,288},{288,32},{64,320},{320,64},{96,352},{352,... | collective-permute-start | bytes 3080 | tf_op jit(solution)/shard_map/ppermute | solution.py:23
  356.3 20.3 %all-to-all-start.2 = ((f32[32,2,128]{2,1,0:T(2,128)}), f32[32,2,128]{2,1,0:T(2,128)S(1)}, u32[]{:S(2)}, u32[]{:S(2)}) async-start(f32[32,2,128]{2,1,0:T(2,128)} %constant_dynamic-update-slice_fusion), calls=%async_computation.2 | async-start | bytes 65536 | tf_op jit(solution)/shard_map/all_to_all | solution.py:11
  623.9 4.3 collective-permute-start.12
  628.2 5.8 collective-permute-start.13
  634.1 4.3 collective-permute-start.14
  638.4 13.8 %collective-permute-start.15 = (f32[2,128]{1,0:T(2,128)S(1)}, f32[2,128]{1,0:T(2,128)S(1)}, u32[]{:S(2)}, u32[]{:S(2)}) collective-permute-start(f32[2,128]{1,0:T(2,128)S(1)} %broadcast_select_fusion.13), channel_id=1, source_target_pairs={{0,256},{256,0},{32,288},{288,32},{64,320},{320,64},{96,352},{352,... | collective-permute-start | bytes 3080 | tf_op jit(solution)/shard_map/ppermute | solution.py:23
  642.2 22.1 %all-to-all-start.3 = ((f32[2,32,128]{2,0,1:T(2,128)}), f32[2,32,128]{2,0,1:T(2,128)S(1)}, u32[]{:S(2)}, u32[]{:S(2)}) async-start(f32[2,32,128]{2,0,1:T(2,128)} %fusion.71), calls=%async_computation.3 | async-start | bytes 65536 | tf_op jit(solution)/shard_map/all_to_all | solution.py:135
  730.3 5.8 collective-permute-start.17
  736.1 4.3 collective-permute-start.18
  740.4 12.5 %collective-permute-start.19 = (f32[2,128]{1,0:T(2,128)S(1)}, f32[2,128]{1,0:T(2,128)S(1)}, u32[]{:S(2)}, u32[]{:S(2)}) collective-permute-start(f32[2,128]{1,0:T(2,128)S(1)} %broadcast_select_fusion.12), channel_id=1, source_target_pairs={{0,256},{256,0},{32,288},{288,32},{64,320},{320,64},{96,352},{352,... | collective-permute-start | bytes 3080 | tf_op jit(solution)/shard_map/ppermute | solution.py:23
  744.5 20.6 %all-to-all-start.4 = ((f32[32,2,128]{2,1,0:T(2,128)}), f32[32,2,128]{2,1,0:T(2,128)S(1)}, u32[]{:S(2)}, u32[]{:S(2)}) async-start(f32[32,2,128]{2,1,0:T(2,128)} %constant_dynamic-update-slice_fusion.32), calls=%async_computation.4 | async-start | bytes 65536 | tf_op jit(solution)/shard_map/all_to_all | solution.py:11
  (23 other events, 675.3 us)
